TPU v7x, 512 devices: a whole 4x4x16 slice. The times are simulated.
512 devices in a mesh: outer: 32 (over y, z_lo, core), inner: 16 (over x, z_hi).
Axes of the slice: x: 4, y: 4, z: 16 (z_hi: 4, z_lo: 4; z = z_hi * 4 + z_lo), core: 2. Of those that a mesh axis runs over, the one named last changes fastest.
Arguments:
- queries: bfloat16 [49152, 2560], P(('outer', 'inner')), may hold values from -120 to 120
- keys: bfloat16 [49152, 2560], P(('outer', 'inner')), may hold values from -4 to 4
- values: bfloat16 [49152, 2560], P(('outer', 'inner')), may hold values from -6 to 6
- doc_start: int32 [49152], P(('outer', 'inner')), may hold values from 0 to 49151, as said below
Outputs:
- attended: bfloat16 [49152, 2560], P(('outer', 'inner'))
Inputs may be any that keep to these rules, and one draw needn't show every extreme that they name: doc_start[p] is the first position of the document that holds p: never decreasing, doc_start[p] <= p, p - doc_start[p] < 480; the first document has exactly (5) * 96 positions.
All inputs are finite; a program needn't handle non-finite values.
Results may differ from a plain program's by a relative error of at most 0.0044.
Values may be sent and summed in bfloat16 or wider, within the bound.
A program may use at most 64 MiB of HBM per device.

v0:
```python
import math

import jax
import jax.numpy as jnp
from jax import lax
from jax.sharding import PartitionSpec as P

HD = 128
SPAN = 6


def passed_along(array, axis, by):
    peers = lax.axis_size(axis)
    pairs = [(i, i + by) for i in range(peers) if 0 <= i + by < peers]
    return lax.ppermute(array, axis, pairs)


def attend(query_rows, key_rows, value_rows, query_pos, key_pos, starts):
    count = query_rows.shape[0]
    heads = query_rows.shape[1] // HD
    group = math.gcd(heads, 4)
    allowed = (key_pos[None, :] >= starts[:, None]) & (key_pos[None, :] <= query_pos[:, None])
    pieces = []
    for first_head in range(0, heads, group):
        low = first_head * HD
        high = (first_head + group) * HD
        query_heads = query_rows[:, low:high].reshape(count, group, HD)
        key_heads = key_rows[:, low:high].reshape(-1, group, HD)
        value_heads = value_rows[:, low:high].reshape(-1, group, HD)
        scores = jnp.einsum(
            "qhd,khd->hqk", query_heads, key_heads, preferred_element_type=jnp.float32
        )
        scores = scores * (1.0 / math.sqrt(HD))
        scores = jnp.where(allowed[None], scores, -jnp.inf)
        largest = jnp.max(scores, axis=-1, keepdims=True)
        expsum = jnp.exp(scores - largest)
        total = jnp.sum(expsum, axis=-1, keepdims=True)
        weights = (expsum / total).astype(jnp.bfloat16)
        mixed = jnp.einsum("hqk,khd->qhd", weights, value_heads, preferred_element_type=jnp.float32)
        pieces.append(mixed.reshape(count, group * HD))
    return jnp.concatenate(pieces, axis=1).astype(jnp.bfloat16)


def body(queries, keys, values, doc_start):
    count = queries.shape[0]
    inner_count = lax.axis_size("inner")
    linear = lax.axis_index("outer") * inner_count + lax.axis_index("inner")
    stacked = jnp.stack([keys, values])
    received = [stacked]
    for offset in range(1, SPAN):
        received.append(passed_along(stacked, ("outer", "inner"), offset))
    ordered = jnp.concatenate(received[::-1], axis=1)
    key_rows = ordered[0]
    value_rows = ordered[1]
    query_pos = linear * count + jnp.arange(count, dtype=jnp.int32)
    key_pos = (linear - (SPAN - 1)) * count + jnp.arange(SPAN * count, dtype=jnp.int32)
    return attend(queries, key_rows, value_rows, query_pos, key_pos, doc_start)


def solution(mesh):
    return jax.shard_map(
        body,
        mesh=mesh,
        in_specs=(
            P(("outer", "inner"), None),
            P(("outer", "inner"), None),
            P(("outer", "inner"), None),
            P(("outer", "inner")),
        ),
        out_specs=P(("outer", "inner"), None),
        check_vma=False,
    )
```

profile of v0, /device:TPU:116, one launch (start us, length us, event | category | flops | bytes accessed | tf_op | source)
XLA Modules:
  0.0 300.1 jit_solution(17981590080664295755)
XLA Ops:
  0.0 1.3 pad_maximum_fusion
  1.3 0.0 copy-start
  1.3 0.0 copy-start.1
  1.3 9.9 %collective-permute-start = (bf16[2,96,2560]{2,1,0:T(8,128)(2,1)S(1)}, bf16[2,96,2560]{2,1,0:T(8,128)(2,1)}, u32[]{:S(2)}, u32[]{:S(2)}) collective-permute-start(bf16[2,96,2560]{2,1,0:T(8,128)(2,1)S(1)} %pad_maximum_fusion), channel_id=1, source_target_pairs={{0,5},{1,6},{2,7},{3,8},{4,9},{5,10},{6,11},{7,12},{8,13},{9,14},{... | collective-permute-start | bytes 2949128 | tf_op jit(solution)/shard_map/ppermute | solution.py:15
  11.2 1.9 collective-permute-start.1
  13.1 3.4 %collective-permute-start.2 = (bf16[2,96,2560]{2,1,0:T(8,128)(2,1)S(1)}, bf16[2,96,2560]{2,1,0:T(8,128)(2,1)}, u32[]{:S(2)}, u32[]{:S(2)}) collective-permute-start(bf16[2,96,2560]{2,1,0:T(8,128)(2,1)S(1)} %pad_maximum_fusion), channel_id=1, source_target_pairs={{0,3},{1,4},{2,5},{3,6},{4,7},{5,8},{6,9},{7,10},{8,11},{9,12},{10... | collective-permute-start | bytes 2949128 | tf_op jit(solution)/shard_map/ppermute | solution.py:15
  16.5 10.8 %collective-permute-start.3 = (bf16[2,96,2560]{2,1,0:T(8,128)(2,1)S(1)}, bf16[2,96,2560]{2,1,0:T(8,128)(2,1)}, u32[]{:S(2)}, u32[]{:S(2)}) collective-permute-start(bf16[2,96,2560]{2,1,0:T(8,128)(2,1)S(1)} %pad_maximum_fusion), channel_id=1, source_target_pairs={{0,2},{1,3},{2,4},{3,5},{4,6},{5,7},{6,8},{7,9},{8,10},{9,11},{10,... | collective-permute-start | bytes 2949128 | tf_op jit(solution)/shard_map/ppermute | solution.py:15
  27.3 4.3 %collective-permute-start.4 = (bf16[2,96,2560]{2,1,0:T(8,128)(2,1)S(1)}, bf16[2,96,2560]{2,1,0:T(8,128)(2,1)S(1)}, u32[]{:S(2)}, u32[]{:S(2)}) collective-permute-start(bf16[2,96,2560]{2,1,0:T(8,128)(2,1)S(1)} %pad_maximum_fusion), channel_id=1, source_target_pairs={{0,1},{1,2},{2,3},{3,4},{4,5},{5,6},{6,7},{7,8},{8,9},{9,10},{10,1... | collective-permute-start | bytes 2949128 | tf_op jit(solution)/shard_map/ppermute | solution.py:15
  31.7 0.8 compare_and_fusion
  32.5 1.1 slice_bitcast_fusion.12
  33.6 128.0 %collective-permute-done = bf16[2,96,2560]{2,1,0:T(8,128)(2,1)} collective-permute-done((bf16[2,96,2560]{2,1,0:T(8,128)(2,1)S(1)}, bf16[2,96,2560]{2,1,0:T(8,128)(2,1)}, u32[]{:S(2)}, u32[]{:S(2)}) %collective-permute-start) | collective-permute-done | bytes 983072 | tf_op jit(solution)/shard_map/ppermute | solution.py:15
  161.5 1.3 constant_dynamic-update-slice_fusion.5
  162.8 0.0 collective-permute-done.1
  162.8 1.3 constant_dynamic-update-slice_fusion.4
  164.1 0.0 collective-permute-done.2
  164.1 1.3 constant_dynamic-update-slice_fusion.3
  165.4 0.0 collective-permute-done.3
  165.4 1.3 constant_dynamic-update-slice_fusion.2
  166.7 109.3 %collective-permute-done.4 = bf16[2,96,2560]{2,1,0:T(8,128)(2,1)S(1)} collective-permute-done((bf16[2,96,2560]{2,1,0:T(8,128)(2,1)S(1)}, bf16[2,96,2560]{2,1,0:T(8,128)(2,1)S(1)}, u32[]{:S(2)}, u32[]{:S(2)}) %collective-permute-start.4) | collective-permute-done | bytes 983072 | tf_op jit(solution)/shard_map/ppermute | solution.py:15
  275.9 0.1 constant_dynamic-update-slice_fusion.1
  276.0 0.0 copy-done
  276.0 0.0 copy-done.1
  276.0 0.1 constant_dynamic-update-slice_fusion
  276.1 0.4 slice_bitcast_fusion.1
  276.5 2.3 slice_bitcast_fusion.2
  278.8 1.3 fusion.16
  280.1 0.6 fusion.120
  280.7 1.4 fusion.18
  282.1 0.6 fusion.115
  282.7 0.4 fusion.20
  283.1 0.6 fusion.110
  283.7 1.3 fusion.22
  285.1 0.6 fusion.105
  285.7 0.4 fusion.24
  286.1 0.6 fusion.100
  286.7 0.0 copy-start.4
  286.7 2.0 fusion.25
  288.7 0.0 copy-start.3
  288.7 0.6 bitcast_dynamic-update-slice_fusion.4
  289.4 2.5 fusion.26
  291.9 0.0 copy-start.2
  291.9 0.7 bitcast_dynamic-update-slice_fusion.3
  292.5 0.0 copy-done.4
  292.5 0.8 fusion.27
  293.4 0.7 bitcast_dynamic-update-slice_fusion.2
  294.0 0.0 copy-done.3
  294.0 2.4 fusion.28
  296.4 0.7 bitcast_dynamic-update-slice_fusion.1
  297.1 0.0 copy-done.2
  297.1 2.3 fusion.29
  299.4 0.7 bitcast_dynamic-update-slice_fusion
  (2 shorter events, 0.0 us)
Async XLA Ops:
  1.3 274.7 %copy-start = (bf16[96,2560]{1,0:T(8,128)(2,1)S(1)}, bf16[96,2560]{1,0:T(8,128)(2,1)}, u32[]{:S(2)}) copy-start(bf16[96,2560]{1,0:T(8,128)(2,1)} %param.6) | copy-start | bytes 1474564
  1.3 274.7 %copy-start.1 = (bf16[96,2560]{1,0:T(8,128)(2,1)S(1)}, bf16[96,2560]{1,0:T(8,128)(2,1)}, u32[]{:S(2)}) copy-start(bf16[96,2560]{1,0:T(8,128)(2,1)} %param.5) | copy-start | bytes 1474564
  1.3 160.2 %collective-permute-start = (bf16[2,96,2560]{2,1,0:T(8,128)(2,1)S(1)}, bf16[2,96,2560]{2,1,0:T(8,128)(2,1)}, u32[]{:S(2)}, u32[]{:S(2)}) collective-permute-start(bf16[2,96,2560]{2,1,0:T(8,128)(2,1)S(1)} %pad_maximum_fusion), channel_id=1, source_target_pairs={{0,5},{1,6},{2,7},{3,8},{4,9},{5,10},{6,11},{7,12},{8,13},{9,14},{... | collective-permute-start | bytes 2949128 | tf_op jit(solution)/shard_map/ppermute | solution.py:15
  11.2 151.7 %collective-permute-start.1 = (bf16[2,96,2560]{2,1,0:T(8,128)(2,1)S(1)}, bf16[2,96,2560]{2,1,0:T(8,128)(2,1)}, u32[]{:S(2)}, u32[]{:S(2)}) collective-permute-start(bf16[2,96,2560]{2,1,0:T(8,128)(2,1)S(1)} %pad_maximum_fusion), channel_id=1, source_target_pairs={{0,4},{1,5},{2,6},{3,7},{4,8},{5,9},{6,10},{7,11},{8,12},{9,13},{1... | collective-permute-start | bytes 2949128 | tf_op jit(solution)/shard_map/ppermute | solution.py:15
  13.1 151.0 %collective-permute-start.2 = (bf16[2,96,2560]{2,1,0:T(8,128)(2,1)S(1)}, bf16[2,96,2560]{2,1,0:T(8,128)(2,1)}, u32[]{:S(2)}, u32[]{:S(2)}) collective-permute-start(bf16[2,96,2560]{2,1,0:T(8,128)(2,1)S(1)} %pad_maximum_fusion), channel_id=1, source_target_pairs={{0,3},{1,4},{2,5},{3,6},{4,7},{5,8},{6,9},{7,10},{8,11},{9,12},{10... | collective-permute-start | bytes 2949128 | tf_op jit(solution)/shard_map/ppermute | solution.py:15
  16.5 148.9 %collective-permute-start.3 = (bf16[2,96,2560]{2,1,0:T(8,128)(2,1)S(1)}, bf16[2,96,2560]{2,1,0:T(8,128)(2,1)}, u32[]{:S(2)}, u32[]{:S(2)}) collective-permute-start(bf16[2,96,2560]{2,1,0:T(8,128)(2,1)S(1)} %pad_maximum_fusion), channel_id=1, source_target_pairs={{0,2},{1,3},{2,4},{3,5},{4,6},{5,7},{6,8},{7,9},{8,10},{9,11},{10,... | collective-permute-start | bytes 2949128 | tf_op jit(solution)/shard_map/ppermute | solution.py:15
  27.3 248.6 %collective-permute-start.4 = (bf16[2,96,2560]{2,1,0:T(8,128)(2,1)S(1)}, bf16[2,96,2560]{2,1,0:T(8,128)(2,1)S(1)}, u32[]{:S(2)}, u32[]{:S(2)}) collective-permute-start(bf16[2,96,2560]{2,1,0:T(8,128)(2,1)S(1)} %pad_maximum_fusion), channel_id=1, source_target_pairs={{0,1},{1,2},{2,3},{3,4},{4,5},{5,6},{6,7},{7,8},{8,9},{9,10},{10,1... | collective-permute-start | bytes 2949128 | tf_op jit(solution)/shard_map/ppermute | solution.py:15
  286.7 5.8 %copy-start.4 = (bf16[72,4,8,128]{3,2,1,0:T(8,128)(2,1)S(1)}, bf16[72,4,8,128]{3,2,1,0:T(8,128)(2,1)}, u32[]{:S(2)}) copy-start(bf16[72,4,8,128]{3,2,1,0:T(8,128)(2,1)} %get-tuple-element.14) | copy-start | bytes 1769476
  288.7 5.3 %copy-start.3 = (bf16[72,4,8,128]{3,2,1,0:T(8,128)(2,1)S(1)}, bf16[72,4,8,128]{3,2,1,0:T(8,128)(2,1)}, u32[]{:S(2)}) copy-start(bf16[72,4,8,128]{3,2,1,0:T(8,128)(2,1)} %get-tuple-element.13) | copy-start | bytes 1769476
  291.9 5.2 %copy-start.2 = (bf16[72,4,8,128]{3,2,1,0:T(8,128)(2,1)S(1)}, bf16[72,4,8,128]{3,2,1,0:T(8,128)(2,1)}, u32[]{:S(2)}) copy-start(bf16[72,4,8,128]{3,2,1,0:T(8,128)(2,1)} %get-tuple-element.12) | copy-start | bytes 1769476
where the time goes:
time: 301 us; the launch traced here: 300 us
  waiting for transfers between devices  237 us (79%)
  starting transfers between devices  30.3 us (10%)
  matrix products  18 us (6%)
  local copies, waits for them, and re-layouts  12.2 us (4%)
    ppermute x5, waiting for transfers between devices, passed_along(): return lax.ppermute(array, axis, pairs)  237 us
    ppermute x5, starting transfers between devices, passed_along(): return lax.ppermute(array, axis, pairs)  30.3 us
    unnamed x21, local copies, waits for them, and re-layouts  11.2 us
    dot_general x5, matrix products, attend(): jnp.einsum('hqk,khd->qhd', weights, value_heads, preferred_element_type=j...  10 us
  transfers between devices with their start and end apart: 5, of which 2 were waited for; matrix products, arithmetic and copies ran while one was open for 2% of the time, Pallas kernels for 0%

commit v1 on v0

v1 whole, which is shorter than its diff:
```python
import functools
import math

import jax
import jax.numpy as jnp
from jax import lax
from jax.experimental import pallas as pl
from jax.experimental.pallas import tpu as pltpu
from jax.sharding import PartitionSpec as P

HD = 128
HEADS = 20
TOK = 96
SPAN = 6
COLS = 4
GROUP = HEADS // COLS
ROW = COLS * TOK
BACK = (SPAN - 1) * TOK
KEYS = BACK + ROW
TILE = 128
WIN = TILE + BACK
SHIFTS = (2, 1, 3)
MESH = pl.DeviceIdType.MESH


def wrap(a, n):
    return lax.rem(a + n, n)


def next_row(o, x, c):
    last = x // 3
    turn = last * (lax.rem(o, 8) // 7)
    return lax.rem(o + last, 32), lax.rem(x + 1, 4), lax.rem(c + turn, COLS)


def prev_row(o, x, c):
    first = (3 - x) // 3
    turn = first * ((7 - lax.rem(o, 8)) // 7)
    return wrap(o - first, 32), wrap(x - 1, 4), wrap(c - turn, COLS)


def device(o, x, c):
    return (o, x * 4 + c)


def kernel(q_ref, k_ref, v_ref, start_ref, out_ref, kv, qb, ob, sb, sc, bias,
           kv_send, kv_recv, q_send, q_recv, o_send, o_recv, x_send, x_recv, s_send, s_recv,
           local):
    o = lax.axis_index("outer")
    inner = lax.axis_index("inner")
    x, c = inner // 4, lax.rem(inner, 4)
    y = o // 8
    mine = wrap(c - y, COLS)
    n1 = next_row(o, x, c)
    n2 = next_row(*n1)
    p1 = prev_row(o, x, c)
    p2 = prev_row(*p1)
    peers = [device(o, x, lax.rem(c + s, COLS)) for s in SHIFTS]
    groups = [lax.rem(mine + s, COLS) for s in SHIFTS]

    barrier = pltpu.get_barrier_semaphore()
    for who in peers + [device(*p1), device(*p2)]:
        pl.semaphore_signal(barrier, inc=1, device_id=who, device_id_type=MESH)

    rows = pl.ds(pl.multiple_of(c * TOK, TOK), TOK)
    own = pl.ds(pl.multiple_of(BACK + c * TOK, TOK), TOK)

    def lanes(group, i):
        return pl.ds(pl.multiple_of(group * (GROUP * HD) + i * HD, HD), HD)

    def local_copies(i):
        return [
            pltpu.make_async_copy(k_ref.at[:, lanes(mine, i)], kv.at[i, 0, own], local.at[0, i]),
            pltpu.make_async_copy(v_ref.at[:, lanes(mine, i)], kv.at[i, 1, own], local.at[1, i]),
            pltpu.make_async_copy(q_ref.at[:, lanes(mine, i)], qb.at[i, rows], local.at[2, i]),
        ]

    def start_copies():
        return [pltpu.make_async_remote_copy(
            src_ref=start_ref, dst_ref=sb.at[c], send_sem=s_send.at[n], recv_sem=s_recv.at[n],
            device_id=peers[n], device_id_type=MESH) for n in range(3)]

    def kv_copies(i):
        return [pltpu.make_async_remote_copy(
            src_ref=ref.at[:, lanes(groups[n], i)], dst_ref=kv.at[i, t, own],
            send_sem=kv_send.at[t, i, n], recv_sem=kv_recv.at[t, i, n],
            device_id=peers[n], device_id_type=MESH)
            for t, ref in enumerate((k_ref, v_ref)) for n in range(3)]

    def q_copies(i):
        return [pltpu.make_async_remote_copy(
            src_ref=q_ref.at[:, lanes(groups[n], i)], dst_ref=qb.at[i, rows],
            send_sem=q_send.at[i, n], recv_sem=q_recv.at[i, n],
            device_id=peers[n], device_id_type=MESH) for n in range(3)]

    def x_copies(i):
        return [
            pltpu.make_async_remote_copy(
                src_ref=kv.at[i, :, pl.ds(BACK, ROW)], dst_ref=kv.at[i, :, pl.ds(TOK, ROW)],
                send_sem=x_send.at[0, i], recv_sem=x_recv.at[0, i],
                device_id=device(*n1), device_id_type=MESH),
            pltpu.make_async_remote_copy(
                src_ref=kv.at[i, :, pl.ds(KEYS - TOK, TOK)], dst_ref=kv.at[i, :, pl.ds(0, TOK)],
                send_sem=x_send.at[1, i], recv_sem=x_recv.at[1, i],
                device_id=device(*n2), device_id_type=MESH),
        ]

    def o_copies(i):
        return [pltpu.make_async_remote_copy(
            src_ref=ob.at[i, pl.ds(pl.multiple_of(lax.rem(c + s, COLS) * TOK, TOK), TOK)],
            dst_ref=out_ref.at[:, lanes(mine, i)],
            send_sem=o_send.at[i, n], recv_sem=o_recv.at[i, n],
            device_id=peers[n], device_id_type=MESH) for n, s in enumerate(SHIFTS)]

    def o_local(i):
        return pltpu.make_async_copy(ob.at[i, rows], out_ref.at[:, lanes(mine, i)], local.at[3, i])

    own_start = pltpu.make_async_copy(start_ref, sb.at[c], local.at[4, 0])
    own_start.start()
    for i in range(GROUP):
        for copy in local_copies(i):
            copy.start()

    pl.semaphore_wait(barrier, 5)
    for copy in start_copies():
        copy.start()
    for i in range(GROUP):
        for copy in kv_copies(i):
            copy.start()
    for i in range(GROUP):
        for copy in q_copies(i):
            copy.start()

    own_start.wait()
    for copy in start_copies():
        copy.wait()
    for b in range(COLS):
        spread = jnp.broadcast_to(sb[b, 0:1, :], (HD, HD)).T
        sc[b * TOK:(b + 1) * TOK, :] = spread[:TOK, :]
    row = o * 4 + x
    for t in range(ROW // TILE):
        first = row * ROW + t * TILE
        key_pos = first - BACK + lax.broadcasted_iota(jnp.int32, (TILE, WIN), 1)
        query_pos = first + lax.broadcasted_iota(jnp.int32, (TILE, WIN), 0)
        starts = sc[t * TILE:(t + 1) * TILE, 0:1]
        allowed = (key_pos >= starts) & (key_pos <= query_pos)
        bias[t] = jnp.where(allowed, 0.0, -jnp.inf)

    @pl.loop(0, GROUP)
    def _(i):
        for copy in local_copies(i)[:2]:
            copy.wait()
        for copy in kv_copies(i):
            copy.wait_recv()
        for copy in x_copies(i):
            copy.start()

    @pl.loop(0, GROUP)
    def _(i):
        local_copies(i)[2].wait()
        for copy in q_copies(i):
            copy.wait_recv()
        for copy in x_copies(i):
            copy.wait_recv()
        for t in range(ROW // TILE):
            low = t * TILE
            scores = lax.dot_general(
                qb[i, low:low + TILE, :], kv[i, 0, low:low + WIN, :],
                (((1,), (1,)), ((), ())), preferred_element_type=jnp.float32)
            scores = scores * (1.0 / math.sqrt(HD)) + bias[t]
            largest = jnp.max(scores, axis=-1, keepdims=True)
            expsum = jnp.exp(scores - largest)
            total = jnp.sum(expsum, axis=-1, keepdims=True)
            weights = (expsum * (1.0 / total)).astype(jnp.bfloat16)
            mixed = jnp.dot(weights, kv[i, 1, low:low + WIN, :], preferred_element_type=jnp.float32)
            ob[i, low:low + TILE, :] = mixed.astype(jnp.bfloat16)
        o_local(i).start()
        for copy in o_copies(i):
            copy.start()

    @pl.loop(0, GROUP)
    def _(i):
        for copy in kv_copies(i) + q_copies(i) + x_copies(i):
            copy.wait_send()
        o_local(i).wait()
        for copy in o_copies(i):
            copy.wait()


def body(queries, keys, values, doc_start):
    starts = jnp.pad(doc_start[None, :], ((0, 7), (0, HD - TOK)))
    width = HEADS * HD
    dma = pltpu.SemaphoreType.DMA
    hbm = pl.BlockSpec(memory_space=pltpu.HBM)
    return pl.pallas_call(
        kernel,
        out_shape=jax.ShapeDtypeStruct((TOK, width), jnp.bfloat16),
        in_specs=[hbm, hbm, hbm, hbm],
        out_specs=hbm,
        scratch_shapes=[
            pltpu.VMEM((GROUP, 2, KEYS, HD), jnp.bfloat16),
            pltpu.VMEM((GROUP, ROW, HD), jnp.bfloat16),
            pltpu.VMEM((GROUP, ROW, HD), jnp.bfloat16),
            pltpu.VMEM((COLS, 8, HD), jnp.int32),
            pltpu.VMEM((ROW, HD), jnp.int32),
            pltpu.VMEM((ROW // TILE, TILE, WIN), jnp.float32),
            dma((2, GROUP, 3)), dma((2, GROUP, 3)),
            dma((GROUP, 3)), dma((GROUP, 3)),
            dma((GROUP, 3)), dma((GROUP, 3)),
            dma((2, GROUP)), dma((2, GROUP)),
            dma((3,)), dma((3,)),
            dma((5, GROUP)),
        ],
        compiler_params=pltpu.CompilerParams(
            collective_id=0, has_side_effects=True, vmem_limit_bytes=32 * 1024 * 1024),
        cost_estimate=pl.CostEstimate(
            flops=4 * TOK * SPAN * TOK * width, bytes_accessed=8 * TOK * width,
            transcendentals=TOK * SPAN * TOK * HEADS),
    )(queries, keys, values, starts)


def solution(mesh):
    rows = P(("outer", "inner"), None)
    return jax.shard_map(
        body,
        mesh=mesh,
        in_specs=(rows, rows, rows, P(("outer", "inner"))),
        out_specs=rows,
        check_vma=False,
    )
```

time: 301 us -> 123 us (0.41)
  the two profiles are of different devices: /device:TPU:116 before, /device:TPU:24 now
where the time goes in v1:
time: 123 us; the launch traced here: 121 us
  Pallas kernels  116 us (94%)
  local copies, waits for them, and re-layouts  4.53 us (4%)
    pallas_call x1, Pallas kernels, body(): pl.pallas_call(kernel, out_shape=jax.ShapeDtypeStruct((TOK, width), jnp.b...  116 us
    unnamed x9, local copies, waits for them, and re-layouts  4.52 us

profile of v1, /device:TPU:24, one launch (start us, length us, event | category | flops | bytes accessed | tf_op | source)
XLA Modules:
  0.0 120.7 jit_solution(12657220083562501053)
XLA Ops:
  0.0 0.0 copy-start.3
  0.0 0.7 copy-done.3
  0.7 0.0 copy-start
  0.7 1.0 copy-done
  1.7 0.0 copy-start.1
  1.7 1.0 copy-done.1
  2.7 0.0 copy-start.2
  2.7 1.0 copy-done.2
  3.8 116.1 %shard_map.46 = bf16[96,2560]{1,0:T(8,128)(2,1)S(1)} custom-call(bf16[96,2560]{1,0:T(8,128)(2,1)S(1)} %copy-done, bf16[96,2560]{1,0:T(8,128)(2,1)S(1)} %copy-done.1, bf16[96,2560]{1,0:T(8,128)(2,1)S(1)} %copy-done.2, s32[8,128]{1,0:T(8,128)S(1)} %pad.4.start_ref), custom_call_target="tpu_custom_call" | custom-call | flops 566231040 | bytes 1966080 | tf_op jit(solution)/shard_map/pallas_call | solution.py:195
  119.9 0.8 copy.6
  (1 shorter events, 0.0 us)
Async XLA Ops:
  0.0 0.7 copy-start.3
  0.7 1.0 copy-start
  1.7 1.0 copy-start.1
  2.7 1.0 copy-start.2

commit v2 on v1

v2 whole, which is shorter than its diff:
```python
import functools
import math

import jax
import jax.numpy as jnp
from jax import lax
from jax.experimental import pallas as pl
from jax.experimental.pallas import tpu as pltpu
from jax.sharding import PartitionSpec as P

HD = 128
HEADS = 20
TOK = 96
SPAN = 6
COLS = 4
GROUP = HEADS // COLS
ROW = COLS * TOK
BACK = (SPAN - 1) * TOK
KEYS = BACK + ROW
TILE = 128
WIN = TILE + BACK
MESH = pl.DeviceIdType.MESH
BF16 = jnp.bfloat16


def wrap(a, n):
    return lax.rem(a + n, n)


def device(x, y, z, core):
    return ((y * 4 + lax.rem(z, 4)) * 2 + core, x * 4 + z // 4)


def row_device(x, y, z, core, by, shift):
    r = core * 4 + x + by + 8
    carry = r // 8 - 1
    r = lax.rem(r, 8)
    z2 = wrap(z + shift, 16)
    at = z2 if by > 0 else z
    y2 = wrap(y + carry * ((3 - lax.rem(at, 4)) // 3), 4)
    return device(lax.rem(r, 4), y2, z2, r // 4)


def kernel(q_ref, k_ref, v_ref, start_ref, out_ref, kv, qb, ob, sb, sc, bias,
           kv_send, kv_recv, q_send, q_recv, o_send, o_recv, x_send, x_recv, s_send, s_recv):
    o = lax.axis_index("outer")
    inner = lax.axis_index("inner")
    x, zh = inner // 4, lax.rem(inner, 4)
    core, zl, y = lax.rem(o, 2), lax.rem(o // 2, 4), o // 8
    z = zh * 4 + zl
    r = core * 4 + x

    def ahead(i):
        return (r + i) // 8

    def along(dz):
        return device(x, y, wrap(z + dz, 16), core)

    def column(i):
        return wrap(z - ahead(i), 16) // 4

    def group(i):
        return wrap(column(i) - y, 4)

    barrier = pltpu.get_barrier_semaphore()
    greeted = [along(-4 * n) for n in (1, 2, 3)]
    greeted += [along(-1 - 4 * n) for n in range(4)] + [along(1 + 4 * n - 16) for n in range(4)]
    greeted += [row_device(x, y, z, core, -by, -shift) for by in (1, 2) for shift in (0, 1)]
    for who in greeted:
        pl.semaphore_signal(barrier, inc=1, device_id=who, device_id_type=MESH)

    rows = pl.ds(pl.multiple_of(zh * TOK, TOK), TOK)
    own = pl.ds(pl.multiple_of(BACK + zh * TOK, TOK), TOK)

    def lanes(g, i):
        return pl.ds(pl.multiple_of(g * (GROUP * HD) + i * HD, HD), HD)

    class Copy:
        def __init__(self, src, dst, send, recv, dz, here):
            self.away = pltpu.make_async_remote_copy(
                src_ref=src, dst_ref=dst, send_sem=send, recv_sem=recv,
                device_id=along(dz), device_id_type=MESH)
            self.home = None if here is None else pltpu.make_async_copy(src, dst, recv)
            self.here = here

        def do(self, away, home):
            if self.here is None:
                away(self.away)
                return
            pl.when(self.here == 0)(lambda: home(self.home))
            pl.when(self.here != 0)(lambda: away(self.away))

        def start(self):
            self.do(lambda c: c.start(), lambda c: c.start())

        def wait_recv(self):
            self.do(lambda c: c.wait_recv(), lambda c: c.wait())

        def wait_send(self):
            self.do(lambda c: c.wait_send(), lambda c: None)

    ORDER = (2, 1, 3, 0)

    def out_lanes(i, n):
        return lanes(wrap(zh + n - y, 4), i)

    def kv_copies(i):
        s = ahead(i)
        return [Copy(ref.at[:, out_lanes(i, n)], kv.at[i, t, own], kv_send.at[t, i, n], kv_recv.at[t, i, n],
                     4 * n + s, s if n == 0 else None)
                for t, ref in enumerate((k_ref, v_ref)) for n in ORDER]

    def q_copies(i):
        s = ahead(i)
        return [Copy(q_ref.at[:, out_lanes(i, n)], qb.at[i, rows], q_send.at[i, n], q_recv.at[i, n],
                     4 * n + s, s if n == 0 else None) for n in ORDER]

    def start_copies():
        return [Copy(start_ref, sb.at[s, zh], s_send.at[s, n], s_recv.at[s, n], 4 * n + s,
                     jnp.int32(0) if n + s == 0 else None) for s in range(2) for n in range(4)]

    def o_copies(i):
        s = ahead(i)
        return [Copy(ob.at[i, pl.ds(pl.multiple_of(wrap(column(i) - n, COLS) * TOK, TOK), TOK)],
                     out_ref.at[:, lanes(group(i), i)], o_send.at[i, n], o_recv.at[i, n],
                     -4 * n - s, s if n == 0 else None) for n in ORDER]

    def x_copies(i):
        copies = []
        for by, src, dst in ((1, pl.ds(BACK, ROW), pl.ds(TOK, ROW)), (2, pl.ds(KEYS - TOK, TOK), pl.ds(0, TOK))):
            there = r + by
            shift = there // 8 + (lax.rem(there, 8) + i) // 8 - ahead(i)
            copies.append(pltpu.make_async_remote_copy(
                src_ref=kv.at[i, :, src], dst_ref=kv.at[i, :, dst],
                send_sem=x_send.at[by - 1, i], recv_sem=x_recv.at[by - 1, i],
                device_id=row_device(x, y, z, core, by, shift), device_id_type=MESH))
        return copies

    pl.semaphore_wait(barrier, len(greeted))
    for copy in start_copies():
        copy.start()
    for i in range(GROUP):
        for copy in kv_copies(i):
            copy.start()
    for i in range(GROUP):
        for copy in q_copies(i):
            copy.start()

    for copy in start_copies():
        copy.wait_recv()
    for s in range(2):
        for b in range(COLS):
            spread = jnp.broadcast_to(sb[s, b, 0:1, :], (HD, HD)).T
            sc[b * TOK:(b + 1) * TOK, :] = spread[:TOK, :]
        row = ((y * 4 + lax.rem(wrap(z - s, 16), 4)) * 2 + core) * 4 + x
        for t in range(ROW // TILE):
            first = row * ROW + t * TILE
            key_pos = first - BACK + lax.broadcasted_iota(jnp.int32, (TILE, WIN), 1)
            query_pos = first + lax.broadcasted_iota(jnp.int32, (TILE, WIN), 0)
            starts = sc[t * TILE:(t + 1) * TILE, 0:1]
            allowed = (key_pos >= starts) & (key_pos <= query_pos)
            bias[s, t] = jnp.where(allowed, 0.0, -jnp.inf)

    @pl.loop(0, GROUP)
    def _(i):
        for copy in kv_copies(i):
            copy.wait_recv()
        for copy in x_copies(i):
            copy.start()

    @pl.loop(0, GROUP)
    def _(i):
        for copy in q_copies(i):
            copy.wait_recv()
        for copy in x_copies(i):
            copy.wait_recv()
        for t in range(ROW // TILE):
            low = t * TILE
            scores = lax.dot_general(
                qb[i, low:low + TILE, :], kv[i, 0, low:low + WIN, :],
                (((1,), (1,)), ((), ())), preferred_element_type=jnp.float32)
            scores = scores * (1.0 / math.sqrt(HD)) + bias[ahead(i), t]
            largest = jnp.max(scores, axis=-1, keepdims=True)
            expsum = jnp.exp(scores - largest)
            total = jnp.sum(expsum, axis=-1, keepdims=True)
            weights = (expsum * (1.0 / total)).astype(BF16)
            mixed = jnp.dot(weights, kv[i, 1, low:low + WIN, :], preferred_element_type=jnp.float32)
            ob[i, low:low + TILE, :] = mixed.astype(BF16)
        for copy in o_copies(i):
            copy.start()

    for copy in start_copies():
        copy.wait_send()

    @pl.loop(0, GROUP)
    def _(i):
        for copy in kv_copies(i) + q_copies(i) + x_copies(i):
            copy.wait_send()
        for copy in o_copies(i):
            copy.wait_recv()
            copy.wait_send()


def body(queries, keys, values, doc_start):
    starts = jnp.pad(doc_start[None, :], ((0, 7), (0, HD - TOK)))
    width = HEADS * HD
    dma = pltpu.SemaphoreType.DMA
    hbm = pl.BlockSpec(memory_space=pltpu.HBM)
    return pl.pallas_call(
        kernel,
        out_shape=jax.ShapeDtypeStruct((TOK, width), jnp.bfloat16),
        in_specs=[hbm, hbm, hbm, hbm],
        out_specs=hbm,
        scratch_shapes=[
            pltpu.VMEM((GROUP, 2, KEYS, HD), jnp.bfloat16),
            pltpu.VMEM((GROUP, ROW, HD), jnp.bfloat16),
            pltpu.VMEM((GROUP, ROW, HD), jnp.bfloat16),
            pltpu.VMEM((2, COLS, 8, HD), jnp.int32),
            pltpu.VMEM((ROW, HD), jnp.int32),
            pltpu.VMEM((2, ROW // TILE, TILE, WIN), jnp.float32),
            dma((2, GROUP, COLS)), dma((2, GROUP, COLS)),
            dma((GROUP, COLS)), dma((GROUP, COLS)),
            dma((GROUP, COLS)), dma((GROUP, COLS)),
            dma((2, GROUP)), dma((2, GROUP)),
            dma((2, COLS)), dma((2, COLS)),
        ],
        compiler_params=pltpu.CompilerParams(
            collective_id=0, has_side_effects=True, vmem_limit_bytes=32 * 1024 * 1024),
        cost_estimate=pl.CostEstimate(
            flops=4 * TOK * SPAN * TOK * width, bytes_accessed=8 * TOK * width,
            transcendentals=TOK * SPAN * TOK * HEADS),
    )(queries, keys, values, starts)


def solution(mesh):
    rows = P(("outer", "inner"), None)
    return jax.shard_map(
        body,
        mesh=mesh,
        in_specs=(rows, rows, rows, P(("outer", "inner"))),
        out_specs=rows,
        check_vma=False,
    )
```

time: 123 us -> 115 us (0.935); the launches traced: 121 us -> 114 us
  Pallas kernels: 116 us -> 110 us
    pallas_call x1, Pallas kernels: 116 us -> 110 us  [body(): pl.pallas_call(kernel, out_shape=jax.ShapeDtypeStruct((TOK, width), jnp.b...]
where the time goes in v2:
time: 115 us; the launch traced here: 114 us
  Pallas kernels  110 us (96%)
  local copies, waits for them, and re-layouts  4.53 us (4%)
    pallas_call x1, Pallas kernels, body(): pl.pallas_call(kernel, out_shape=jax.ShapeDtypeStruct((TOK, width), jnp.b...  110 us
    unnamed x9, local copies, waits for them, and re-layouts  4.52 us

profile of v2, /device:TPU:24, one launch (start us, length us, event | category | flops | bytes accessed | tf_op | source)
XLA Modules:
  0.0 114.3 jit_solution(626075113292064278)
XLA Ops:
  0.0 0.0 copy-start.3
  0.0 0.7 copy-done.3
  0.7 0.0 copy-start
  0.7 1.0 copy-done
  1.7 0.0 copy-start.1
  1.7 1.0 copy-done.1
  2.7 0.0 copy-start.2
  2.7 1.0 copy-done.2
  3.8 109.8 %shard_map.46 = bf16[96,2560]{1,0:T(8,128)(2,1)S(1)} custom-call(bf16[96,2560]{1,0:T(8,128)(2,1)S(1)} %copy-done, bf16[96,2560]{1,0:T(8,128)(2,1)S(1)} %copy-done.1, bf16[96,2560]{1,0:T(8,128)(2,1)S(1)} %copy-done.2, s32[8,128]{1,0:T(8,128)S(1)} %pad.4.start_ref), custom_call_target="tpu_custom_call" | custom-call | flops 566231040 | bytes 1966080 | tf_op jit(solution)/shard_map/pallas_call | solution.py:209
  113.5 0.8 copy.6
  (1 shorter events, 0.0 us)
Async XLA Ops:
  0.0 0.7 copy-start.3
  0.7 1.0 copy-start
  1.7 1.0 copy-start.1
  2.7 1.0 copy-start.2

commit v3 on v2

--- a/solution.py
+++ b/solution.py
@@ -17,8 +17,8 @@
 ROW = COLS * TOK
 BACK = (SPAN - 1) * TOK
 KEYS = BACK + ROW
-TILE = 128
-WIN = TILE + BACK
+WIN = SPAN * TOK
+LAST = 2
 MESH = pl.DeviceIdType.MESH
 BF16 = jnp.bfloat16
 
@@ -101,29 +101,35 @@
 
     ORDER = (2, 1, 3, 0)
 
-    def out_lanes(i, n):
-        return lanes(wrap(zh + n - y, 4), i)
-
     def kv_copies(i):
         s = ahead(i)
-        return [Copy(ref.at[:, out_lanes(i, n)], kv.at[i, t, own], kv_send.at[t, i, n], kv_recv.at[t, i, n],
-                     4 * n + s, s if n == 0 else None)
+        return [Copy(ref.at[:, lanes(wrap(zh + n - y, 4), i)], kv.at[i, t, own],
+                     kv_send.at[t, i, n], kv_recv.at[t, i, n], 4 * n + s, s if n == 0 else None)
                 for t, ref in enumerate((k_ref, v_ref)) for n in ORDER]
 
-    def q_copies(i):
+    def q_copy(i, to):
+        s, n = ahead(i), wrap(to - zh, COLS)
+        return Copy(q_ref.at[:, lanes(wrap(to - y, COLS), i)], qb.at[i, rows], q_send.at[i, n], q_recv.at[i, n],
+                    4 * n + s, n + s)
+
+    def q_here(i, b):
+        s, n = ahead(i), wrap(column(i) - b, COLS)
+        return Copy(q_ref.at[:, lanes(group(i), i)], qb.at[i, pl.ds(pl.multiple_of(b * TOK, TOK), TOK)],
+                    q_send.at[i, n], q_recv.at[i, n], -4 * n - s, n + s)
+
+    def o_copy(i, b):
+        s, n = ahead(i), wrap(column(i) - b, COLS)
+        return Copy(ob.at[i, pl.ds(pl.multiple_of(b * TOK, TOK), TOK)], out_ref.at[:, lanes(group(i), i)],
+                    o_send.at[i, n], o_recv.at[i, n], -4 * n - s, n + s)
+
+    def o_here(i, n):
         s = ahead(i)
-        return [Copy(q_ref.at[:, out_lanes(i, n)], qb.at[i, rows], q_send.at[i, n], q_recv.at[i, n],
-                     4 * n + s, s if n == 0 else None) for n in ORDER]
+        return Copy(ob.at[i, rows], out_ref.at[:, lanes(wrap(zh + n - y, COLS), i)],
+                    o_send.at[i, n], o_recv.at[i, n], 4 * n + s, s if n == 0 else None)
 
     def start_copies():
         return [Copy(start_ref, sb.at[s, zh], s_send.at[s, n], s_recv.at[s, n], 4 * n + s,
                      jnp.int32(0) if n + s == 0 else None) for s in range(2) for n in range(4)]
-
-    def o_copies(i):
-        s = ahead(i)
-        return [Copy(ob.at[i, pl.ds(pl.multiple_of(wrap(column(i) - n, COLS) * TOK, TOK), TOK)],
-                     out_ref.at[:, lanes(group(i), i)], o_send.at[i, n], o_recv.at[i, n],
-                     -4 * n - s, s if n == 0 else None) for n in ORDER]
 
     def x_copies(i):
         copies = []
@@ -142,24 +148,29 @@
     for i in range(GROUP):
         for copy in kv_copies(i):
             copy.start()
-    for i in range(GROUP):
-        for copy in q_copies(i):
-            copy.start()
+    for i in range(GROUP - LAST):
+        for to in range(COLS):
+            q_copy(i, to).start()
+    for to in range(COLS):
+        for i in range(GROUP - LAST, GROUP):
+            q_copy(i, to).start()
 
     for copy in start_copies():
         copy.wait_recv()
+    diagonal = lax.broadcasted_iota(jnp.int32, (TOK, TOK), 0) == lax.broadcasted_iota(jnp.int32, (TOK, TOK), 1)
     for s in range(2):
         for b in range(COLS):
-            spread = jnp.broadcast_to(sb[s, b, 0:1, :], (HD, HD)).T
-            sc[b * TOK:(b + 1) * TOK, :] = spread[:TOK, :]
+            spread = jnp.broadcast_to(sb[s, b].astype(jnp.float32), (TOK, TOK))
+            down = jnp.sum(jnp.where(diagonal, spread, 0.0), axis=1, keepdims=True)
+            sc[b * TOK:(b + 1) * TOK, :] = jnp.broadcast_to(down.astype(jnp.int32), (TOK, HD))
         row = ((y * 4 + lax.rem(wrap(z - s, 16), 4)) * 2 + core) * 4 + x
-        for t in range(ROW // TILE):
-            first = row * ROW + t * TILE
-            key_pos = first - BACK + lax.broadcasted_iota(jnp.int32, (TILE, WIN), 1)
-            query_pos = first + lax.broadcasted_iota(jnp.int32, (TILE, WIN), 0)
-            starts = sc[t * TILE:(t + 1) * TILE, 0:1]
+        for b in range(COLS):
+            first = row * ROW + b * TOK
+            key_pos = first - BACK + lax.broadcasted_iota(jnp.int32, (TOK, WIN), 1)
+            query_pos = first + lax.broadcasted_iota(jnp.int32, (TOK, WIN), 0)
+            starts = sc[b * TOK:(b + 1) * TOK, 0:1]
             allowed = (key_pos >= starts) & (key_pos <= query_pos)
-            bias[s, t] = jnp.where(allowed, 0.0, -jnp.inf)
+            bias[s, b] = jnp.where(allowed, 0.0, -jnp.inf)
 
     @pl.loop(0, GROUP)
     def _(i):
@@ -168,41 +179,58 @@
         for copy in x_copies(i):
             copy.start()
 
+    def block(i, b):
+        q_here(i, b).wait_recv()
+        low = pl.multiple_of(b * TOK, TOK)
+        scores = lax.dot_general(
+            qb[i, pl.ds(low, TOK), :], kv[i, 0, pl.ds(low, WIN), :],
+            (((1,), (1,)), ((), ())), preferred_element_type=jnp.float32)
+        scores = scores * (1.0 / math.sqrt(HD)) + bias[ahead(i), b]
+        largest = jnp.max(scores, axis=-1, keepdims=True)
+        expsum = jnp.exp(scores - largest)
+        total = jnp.sum(expsum, axis=-1, keepdims=True)
+        weights = (expsum * (1.0 / total)).astype(BF16)
+        mixed = jnp.dot(weights, kv[i, 1, pl.ds(low, WIN), :], preferred_element_type=jnp.float32)
+        ob[i, pl.ds(low, TOK), :] = mixed.astype(BF16)
+        o_copy(i, b).start()
+
+    @pl.loop(0, GROUP - LAST)
+    def _(i):
+        for copy in x_copies(i):
+            copy.wait_recv()
+
+        @pl.loop(0, COLS)
+        def _(b):
+            block(i, b)
+
+    for i in range(GROUP - LAST, GROUP):
+        for copy in x_copies(i):
+            copy.wait_recv()
+
+    @pl.loop(0, COLS)
+    def _(b):
+        @pl.loop(GROUP - LAST, GROUP)
+        def _(i):
+            block(i, b)
+
+    for copy in start_copies():
+        copy.wait_send()
+
     @pl.loop(0, GROUP)
     def _(i):
-        for copy in q_copies(i):
-            copy.wait_recv()
-        for copy in x_copies(i):
-            copy.wait_recv()
-        for t in range(ROW // TILE):
-            low = t * TILE
-            scores = lax.dot_general(
-                qb[i, low:low + TILE, :], kv[i, 0, low:low + WIN, :],
-                (((1,), (1,)), ((), ())), preferred_element_type=jnp.float32)
-            scores = scores * (1.0 / math.sqrt(HD)) + bias[ahead(i), t]
-            largest = jnp.max(scores, axis=-1, keepdims=True)
-            expsum = jnp.exp(scores - largest)
-            total = jnp.sum(expsum, axis=-1, keepdims=True)
-            weights = (expsum * (1.0 / total)).astype(BF16)
-            mixed = jnp.dot(weights, kv[i, 1, low:low + WIN, :], preferred_element_type=jnp.float32)
-            ob[i, low:low + TILE, :] = mixed.astype(BF16)
-        for copy in o_copies(i):
-            copy.start()
-
-    for copy in start_copies():
-        copy.wait_send()
-
-    @pl.loop(0, GROUP)
-    def _(i):
-        for copy in kv_copies(i) + q_copies(i) + x_copies(i):
+        for copy in kv_copies(i) + x_copies(i):
             copy.wait_send()
-        for copy in o_copies(i):
-            copy.wait_recv()
-            copy.wait_send()
+        for n in range(COLS):
+            o_here(i, n).wait_recv()
+
+        @pl.loop(0, COLS)
+        def _(b):
+            q_copy(i, b).wait_send()
+            o_copy(i, b).wait_send()
 
 
 def body(queries, keys, values, doc_start):
-    starts = jnp.pad(doc_start[None, :], ((0, 7), (0, HD - TOK)))
+    starts = doc_start.reshape(1, TOK)
     width = HEADS * HD
     dma = pltpu.SemaphoreType.DMA
     hbm = pl.BlockSpec(memory_space=pltpu.HBM)
@@ -215,9 +243,9 @@
             pltpu.VMEM((GROUP, 2, KEYS, HD), jnp.bfloat16),
             pltpu.VMEM((GROUP, ROW, HD), jnp.bfloat16),
             pltpu.VMEM((GROUP, ROW, HD), jnp.bfloat16),
-            pltpu.VMEM((2, COLS, 8, HD), jnp.int32),
+            pltpu.VMEM((2, COLS, 1, TOK), jnp.int32),
             pltpu.VMEM((ROW, HD), jnp.int32),
-            pltpu.VMEM((2, ROW // TILE, TILE, WIN), jnp.float32),
+            pltpu.VMEM((2, COLS, TOK, WIN), jnp.float32),
             dma((2, GROUP, COLS)), dma((2, GROUP, COLS)),
             dma((GROUP, COLS)), dma((GROUP, COLS)),
             dma((GROUP, COLS)), dma((GROUP, COLS)),
@@ -225,7 +253,7 @@
             dma((2, COLS)), dma((2, COLS)),
         ],
         compiler_params=pltpu.CompilerParams(
-            collective_id=0, has_side_effects=True, vmem_limit_bytes=32 * 1024 * 1024),
+            collective_id=0, has_side_effects=True, vmem_limit_bytes=60 * 1024 * 1024),
         cost_estimate=pl.CostEstimate(
             flops=4 * TOK * SPAN * TOK * width, bytes_accessed=8 * TOK * width,
             transcendentals=TOK * SPAN * TOK * HEADS),

time: 115 us -> 109 us (0.948); the launches traced: 114 us -> 107 us
  Pallas kernels: 110 us -> 105 us
  local copies, waits for them, and re-layouts: 4.53 us -> 1.84 us
    pallas_call x1, Pallas kernels: 110 us -> 105 us  [body(): pl.pallas_call(kernel, out_shape=jax.ShapeDtypeStruct((TOK, width), jnp.b...]
    unnamed x9 -> x1, local copies, waits for them, and re-layouts: 4.52 us -> 1.84 us
where the time goes in v3:
time: 109 us; the launch traced here: 107 us
  Pallas kernels  105 us (96%)
  local copies, waits for them, and re-layouts  1.84 us (2%)
    pallas_call x1, Pallas kernels, body(): pl.pallas_call(kernel, out_shape=jax.ShapeDtypeStruct((TOK, width), jnp.b...  105 us

profile of v3, /device:TPU:24, one launch (start us, length us, event | category | flops | bytes accessed | tf_op | source)
XLA Modules:
  0.0 107.0 jit_solution(11413753447128326111)
XLA Ops:
  0.0 105.2 %shard_map.46 = bf16[96,2560]{1,0:T(8,128)(2,1)} custom-call(bf16[96,2560]{1,0:T(8,128)(2,1)} %q_ref.1, bf16[96,2560]{1,0:T(8,128)(2,1)} %k_ref.1, bf16[96,2560]{1,0:T(8,128)(2,1)} %v_ref.1, s32[1,96]{1,0:T(1,128)} %bitcast.1), custom_call_target="tpu_custom_call" | custom-call | flops 566231040 | bytes 1966080 | tf_op jit(solution)/shard_map/pallas_call | solution.py:237
  105.2 1.8 %copy.6 = bf16[96,2560]{1,0:T(8,128)(2,1)} copy(bf16[96,2560]{1,0:T(8,128)(2,1)} %shard_map.46) | data formatting | bytes 983040

commit v4 on v3

--- a/solution.py
+++ b/solution.py
@@ -143,17 +143,11 @@
         return copies
 
     pl.semaphore_wait(barrier, len(greeted))
-    for copy in start_copies():
+    for copy in kv_copies(0) + start_copies():
         copy.start()
-    for i in range(GROUP):
+    for i in range(1, GROUP):
         for copy in kv_copies(i):
             copy.start()
-    for i in range(GROUP - LAST):
-        for to in range(COLS):
-            q_copy(i, to).start()
-    for to in range(COLS):
-        for i in range(GROUP - LAST, GROUP):
-            q_copy(i, to).start()
 
     for copy in start_copies():
         copy.wait_recv()
@@ -172,12 +166,20 @@
             allowed = (key_pos >= starts) & (key_pos <= query_pos)
             bias[s, b] = jnp.where(allowed, 0.0, -jnp.inf)
 
-    @pl.loop(0, GROUP)
-    def _(i):
+    def pass_on(i):
         for copy in kv_copies(i):
             copy.wait_recv()
         for copy in x_copies(i):
             copy.start()
+
+    pass_on(0)
+    for i in range(GROUP - LAST):
+        for to in range(COLS):
+            q_copy(i, to).start()
+    for to in range(COLS):
+        for i in range(GROUP - LAST, GROUP):
+            q_copy(i, to).start()
+    pl.loop(1, GROUP)(pass_on)
 
     def block(i, b):
         q_here(i, b).wait_recv()

time: 109 us -> 109 us (level)
  no operation moved by 1% of the time
where the time goes in v4:
time: 109 us; the launch traced here: 107 us
  Pallas kernels  105 us (96%)
  local copies, waits for them, and re-layouts  1.84 us (2%)
    pallas_call x1, Pallas kernels, body(): pl.pallas_call(kernel, out_shape=jax.ShapeDtypeStruct((TOK, width), jnp.b...  105 us

profile of v4, /device:TPU:24, one launch (start us, length us, event | category | flops | bytes accessed | tf_op | source)
XLA Modules:
  0.0 107.2 jit_solution(17709372677318391688)
XLA Ops:
  0.0 105.3 %shard_map.46 = bf16[96,2560]{1,0:T(8,128)(2,1)} custom-call(bf16[96,2560]{1,0:T(8,128)(2,1)} %q_ref.1, bf16[96,2560]{1,0:T(8,128)(2,1)} %k_ref.1, bf16[96,2560]{1,0:T(8,128)(2,1)} %v_ref.1, s32[1,96]{1,0:T(1,128)} %bitcast.1), custom_call_target="tpu_custom_call" | custom-call | flops 566231040 | bytes 1966080 | tf_op jit(solution)/shard_map/pallas_call | solution.py:239
  105.3 1.8 %copy.6 = bf16[96,2560]{1,0:T(8,128)(2,1)} copy(bf16[96,2560]{1,0:T(8,128)(2,1)} %shard_map.46) | data formatting | bytes 983040
